TPU v7x, 32 devices: a whole 2x2x4 slice. The times are simulated.
32 devices in a mesh: slab: 8 (over z, y), blk: 4 (over x, core).
Axes of the slice: x: 2, y: 2, z: 4, core: 2. Of those that a mesh axis runs over, the one named last changes fastest.
Arguments:
- positions: float32 [1024, 3, 128], P(('slab', 'blk')), may hold values from 0 to 1
- radius: float32 [1024, 128], P(('slab', 'blk')), may hold values from 0.15 to 0.3
- velocity: float32 [1024, 3, 128], P(('slab', 'blk')), may hold values from -3 to 3
- old_force: float32 [1024, 3, 128], P(('slab', 'blk')), may hold values from -6 to 6
- neighbours: int32 [1024, 16], P(('slab', 'blk')), may hold values from 0 to 47, as said below
- tile_count: int32 [1024], P(('slab', 'blk')), may hold values from 0 to 16
Outputs:
- new_positions: float32 [1024, 3, 128], P(('slab', 'blk'))
- new_velocity: float32 [1024, 3, 128], P(('slab', 'blk'))
- new_force: float32 [1024, 3, 128], P(('slab', 'blk'))
Inputs may be any that keep to these rules, and one draw needn't show every extreme that they name: neighbours[i, k] indexes the candidate list of bin i's group; it never names bin i itself, and names no candidate of a missing slab at the drum's ends.
All inputs are finite; a program needn't handle non-finite values.
Results may differ from a plain program's by a relative error of at most 0.0003.
Values sent between devices are 32-bit elements; how exact they have to be, the bound alone decides.
A program may use at most 64 MiB of HBM per device.

v0:
```python
import functools

import jax
import jax.numpy as jnp
from jax import lax
from jax.experimental import pallas as pl
from jax.experimental.pallas import tpu as pltpu
from jax.sharding import PartitionSpec as P

GHOSTS = 8
STIFFNESS = 10.0
SOFTENING = 0.0025
TIMESTEP = 0.2
TINY = 1e-30
BIN_COST = 3
MESH = pl.DeviceIdType.MESH


def acceleration(force, radius):
    accel = force / (125.0 * radius * radius * radius)
    component = lax.broadcasted_iota(jnp.int32, accel.shape, 1)
    return accel + jnp.where(component == 1, -0.5, 0.0)


def greet(slabs, sectors):
    slab, sector = lax.axis_index("slab"), lax.axis_index("blk")
    barrier = pltpu.get_barrier_semaphore()
    for step in range(1, sectors):
        other = lax.rem(sector + step, sectors)
        pl.semaphore_signal(barrier, inc=1, device_id=(slab, other), device_id_type=MESH)

    @pl.when(slab > 0)
    def _():
        for step in range(sectors):
            other = lax.rem(sector + step, sectors)
            pl.semaphore_signal(barrier, inc=1, device_id=(slab - 1, other), device_id_type=MESH)

    @pl.when(slab < slabs - 1)
    def _():
        for step in range(sectors):
            other = lax.rem(sector + step, sectors)
            pl.semaphore_signal(barrier, inc=1, device_id=(slab + 1, other), device_id_type=MESH)

    beside = jnp.where(slab > 0, sectors, 0) + jnp.where(slab < slabs - 1, sectors, 0)
    pl.semaphore_wait(barrier, sectors - 1 + beside)


def spread_kernel(
    slabs, sectors, pos_in, rad_in, vel_in, old_in, neigh_in, count_in,
    ext, neigh_all, count_all, base, mass, pos, rad, vel, old, send, recv, local,
):
    slab, sector = lax.axis_index("slab"), lax.axis_index("blk")
    bins = pos.shape[0]
    fetches = [
        pltpu.make_async_copy(source, target, local.at[index])
        for index, (source, target) in enumerate((
            (pos_in, pos), (rad_in, rad), (vel_in, vel), (old_in, old),
            (neigh_in, neigh_all.at[sector]), (count_in, count_all.at[sector]),
        ))
    ]
    for fetch in fetches:
        fetch.start()
    greet(slabs, sectors)
    for fetch in fetches:
        fetch.wait()
    radius = rad[...][:, None, :]
    accel_old = acceleration(old[...], radius)
    moved = pos[...] + TIMESTEP * vel[...] + 0.5 * TIMESTEP * TIMESTEP * accel_old
    ext[sector, pl.ds(GHOSTS, bins), 0:3, :] = moved
    ext[sector, pl.ds(GHOSTS, bins), 3:4, :] = radius

    def mate(step, what):
        other = lax.rem(sector + step, sectors)
        ref = (ext.at[sector, pl.ds(GHOSTS, bins)], neigh_all.at[sector], count_all.at[sector])[what]
        return pltpu.make_async_remote_copy(
            src_ref=ref, dst_ref=ref, send_sem=send.at[what, step], recv_sem=recv.at[what, step],
            device_id=(slab, other), device_id_type=MESH,
        )

    def beside(step, up):
        other = lax.rem(sector + step, sectors)
        own_first = bins if up else GHOSTS
        there = 0 if up else GHOSTS + bins
        return pltpu.make_async_remote_copy(
            src_ref=ext.at[sector, pl.ds(own_first, GHOSTS)],
            dst_ref=ext.at[sector, pl.ds(there, GHOSTS)],
            send_sem=send.at[3 + up, step], recv_sem=recv.at[3 + up, step],
            device_id=(slab + (1 if up else -1), other), device_id_type=MESH,
        )

    for step in range(1, sectors):
        for what in range(3):
            mate(step, what).start()

    @pl.when(slab > 0)
    def _():
        for step in range(sectors):
            beside(step, 0).start()

    @pl.when(slab < slabs - 1)
    def _():
        for step in range(sectors):
            beside(step, 1).start()

    base[...] = vel[...] + 0.5 * TIMESTEP * accel_old
    mass[...] = 125.0 * radius * radius * radius
    for step in range(1, sectors):
        for what in range(3):
            mate(step, what).wait()

    @pl.when(slab > 0)
    def _():
        for step in range(sectors):
            beside(step, 0).wait_send()
            beside(step, 1).wait_recv()

    @pl.when(slab < slabs - 1)
    def _():
        for step in range(sectors):
            beside(step, 1).wait_send()
            beside(step, 0).wait_recv()


def tiles_kernel(sectors, neigh, count, ext, moved_out, react, acol, acc, moved, done):
    sector = lax.axis_index("blk")
    bins = neigh.shape[1]
    spheres = ext.shape[3]
    strips = spheres // 8
    moved[...] = ext[sector, pl.ds(GHOSTS, bins), 0:3, :]
    store = pltpu.make_async_copy(moved, moved_out, done)
    store.start()
    react[...] = jnp.zeros_like(react)
    diagonal = lax.broadcasted_iota(jnp.int32, (spheres, spheres), 0) == lax.broadcasted_iota(
        jnp.int32, (spheres, spheres), 1
    )

    def group_units(group):
        return lax.fori_loop(
            0, bins, lambda own, t: t + count[group, 0, own] + BIN_COST, 0, unroll=bins
        )

    sizes = [group_units(group) for group in range(sectors)]
    total = sum(sizes)
    first = total * sector // sectors
    last = total * (sector + 1) // sectors

    def pair(others, both):
        rows_of = []
        for other in others:
            row = [jnp.broadcast_to(other[c : c + 1, :], (8, spheres)) for c in range(4)]
            rows_of.append(row + [0.01 / row[3]])
        totals = [[None] * 3 for _ in others]
        for strip in range(strips):
            rows = pl.ds(8 * strip, 8)
            column = [acol[c, rows, :] for c in range(5)]
            sums = [None] * 3
            for row, total_b in zip(rows_of, totals):
                d = [column[c] - row[c] for c in range(3)]
                square = d[0] * d[0] + d[1] * d[1] + (d[2] * d[2] + SOFTENING)
                inverse = lax.rsqrt(square)
                overlap = jnp.maximum(column[3] + row[3] - square * inverse, TINY)
                stiff = lax.rsqrt(overlap * (column[4] + row[4]))
                pull = overlap * overlap * (inverse * stiff)
                for c in range(3):
                    w = pull * d[c]
                    total_b[c] = w if strip == 0 else total_b[c] + w
                    sums[c] = w if sums[c] is None else sums[c] + w
            if both:
                for c in range(3):
                    acc[c, rows, :] += sums[c]
        return [
            jnp.concatenate([jnp.sum(t, axis=0, keepdims=True) for t in total_b], axis=0)
            for total_b in totals
        ]

    def one_bin(group, own, start):
        tiles = count[group, 0, own]
        units = tiles + BIN_COST
        low = jnp.maximum(first - start - BIN_COST, 0)
        high = jnp.minimum(last - start - BIN_COST, tiles)
        alone = (start >= first) & (start < last)

        @pl.when((high > low) | alone)
        def _():
            mine = ext[group, GHOSTS + own]
            wide = jnp.concatenate([mine, 0.01 / mine], axis=0).T
            for c, column in enumerate((0, 1, 2, 3, 7)):
                acol[c] = jnp.broadcast_to(wide[:, column : column + 1], (spheres, spheres))

            @pl.when(alone)
            def _():
                react[group, GHOSTS + own] -= pair([mine], False)[0]

            @pl.when(high > low)
            def _():
                acc[...] = jnp.zeros_like(acc)
                twos = (high - low) // 2

                def two_tiles(k, _):
                    one = neigh[group, own, low + 2 * k]
                    two = neigh[group, own, low + 2 * k + 1]
                    forces = pair([ext[group, one], ext[group, two]], True)
                    react[group, one] -= forces[0]
                    react[group, two] -= forces[1]
                    return 0

                lax.fori_loop(0, twos, two_tiles, 0)

                @pl.when(low + 2 * twos < high)
                def _():
                    one = neigh[group, own, high - 1]
                    react[group, one] -= pair([ext[group, one]], True)[0]

                react[group, GHOSTS + own] += jnp.concatenate(
                    [
                        jnp.sum(
                            jnp.where(diagonal, jnp.sum(acc[c], axis=1, keepdims=True), 0.0),
                            axis=0, keepdims=True,
                        )
                        for c in range(3)
                    ],
                    axis=0,
                )

        return start + units

    def one_group(group, start):
        stop = start
        for other in range(sectors):
            stop += jnp.where(group == other, sizes[other], 0)
        touched = (stop > first) & (start < last)
        lax.fori_loop(
            0, jnp.where(touched, bins, 0), functools.partial(one_bin, group), start
        )
        return stop

    lax.fori_loop(0, sectors, one_group, 0)
    store.wait()


def gather_kernel(slabs, sectors, bins, react, total, mates, below, above, send, recv):
    slab, sector = lax.axis_index("slab"), lax.axis_index("blk")
    greet(slabs, sectors)

    def mate(step):
        other = lax.rem(sector + step, sectors)
        return pltpu.make_async_remote_copy(
            src_ref=react.at[other, pl.ds(GHOSTS, bins)], dst_ref=mates.at[step],
            send_sem=send.at[0, step], recv_sem=recv.at[0, step],
            device_id=(slab, other), device_id_type=MESH,
        )

    def beside(step, up):
        other = lax.rem(sector + step, sectors)
        return pltpu.make_async_remote_copy(
            src_ref=react.at[other, pl.ds(GHOSTS + bins if up else 0, GHOSTS)],
            dst_ref=(below if up else above).at[step],
            send_sem=send.at[1 + up, step], recv_sem=recv.at[1 + up, step],
            device_id=(slab + (1 if up else -1), other), device_id_type=MESH,
        )

    for step in range(1, sectors):
        mate(step).start()

    @pl.when(slab > 0)
    def _():
        for step in range(sectors):
            beside(step, 0).start()

    @pl.when(slab < slabs - 1)
    def _():
        for step in range(sectors):
            beside(step, 1).start()

    total[...] = react[sector, pl.ds(GHOSTS, bins)]
    for step in range(1, sectors):
        mate(step).wait()
        total[...] += mates[step]

    @pl.when(slab > 0)
    def _():
        for step in range(sectors):
            beside(step, 0).wait_send()
            beside(step, 1).wait_recv()
            total[0:GHOSTS] += below[step]

    @pl.when(slab < slabs - 1)
    def _():
        for step in range(sectors):
            beside(step, 1).wait_send()
            beside(step, 0).wait_recv()
            total[pl.ds(bins - GHOSTS, GHOSTS)] += above[step]


def finish_kernel(force, base, mass, velocity_out, force_out, velocity, done):
    copy_force = pltpu.make_async_copy(force, force_out, done.at[0])
    copy_force.start()
    component = lax.broadcasted_iota(jnp.int32, force.shape, 1)
    accel = force[...] / mass[...] + jnp.where(component == 1, -0.5, 0.0)
    velocity[...] = base[...] + 0.5 * TIMESTEP * accel
    copy_velocity = pltpu.make_async_copy(velocity, velocity_out, done.at[1])
    copy_velocity.start()
    copy_force.wait()
    copy_velocity.wait()


def solution(mesh):
    slabs, sectors = mesh.shape["slab"], mesh.shape["blk"]
    vmem = pl.BlockSpec(memory_space=pltpu.VMEM)
    smem = pl.BlockSpec(memory_space=pltpu.SMEM)
    hbm = pl.BlockSpec(memory_space=pltpu.HBM)

    def local(positions, radius, velocity, old_force, neighbours, tile_count):
        bins, _, spheres = positions.shape
        slots = neighbours.shape[1]
        candidates = bins + 2 * GHOSTS
        ext, neigh_all, count_all, base, mass = pl.pallas_call(
            functools.partial(spread_kernel, slabs, sectors),
            out_shape=(
                jax.ShapeDtypeStruct((sectors, candidates, 4, spheres), jnp.float32),
                jax.ShapeDtypeStruct((sectors, bins, slots), jnp.int32),
                jax.ShapeDtypeStruct((sectors, 1, bins), jnp.int32),
                jax.ShapeDtypeStruct((bins, 3, spheres), jnp.float32),
                jax.ShapeDtypeStruct((bins, 1, spheres), jnp.float32),
            ),
            in_specs=[hbm] * 6,
            out_specs=(vmem,) * 5,
            scratch_shapes=[
                pltpu.VMEM((bins, 3, spheres), jnp.float32),
                pltpu.VMEM((bins, spheres), jnp.float32),
                pltpu.VMEM((bins, 3, spheres), jnp.float32),
                pltpu.VMEM((bins, 3, spheres), jnp.float32),
                pltpu.SemaphoreType.DMA((5, sectors)),
                pltpu.SemaphoreType.DMA((5, sectors)),
                pltpu.SemaphoreType.DMA((6,)),
            ],
            compiler_params=pltpu.CompilerParams(
                collective_id=0, has_side_effects=True, vmem_limit_bytes=32 * 2**20
            ),
        )(positions, radius, velocity, old_force, neighbours, tile_count.reshape(1, bins))
        moved, react = pl.pallas_call(
            functools.partial(tiles_kernel, sectors),
            out_shape=(
                jax.ShapeDtypeStruct((bins, 3, spheres), jnp.float32),
                jax.ShapeDtypeStruct((sectors, candidates, 3, spheres), jnp.float32),
            ),
            in_specs=[smem, smem, vmem],
            out_specs=(hbm, vmem),
            scratch_shapes=[
                pltpu.VMEM((5, spheres, spheres), jnp.float32),
                pltpu.VMEM((3, spheres, spheres), jnp.float32),
                pltpu.VMEM((bins, 3, spheres), jnp.float32),
                pltpu.SemaphoreType.DMA,
            ],
            compiler_params=pltpu.CompilerParams(vmem_limit_bytes=32 * 2**20),
        )(neigh_all, count_all, ext)
        force = pl.pallas_call(
            functools.partial(gather_kernel, slabs, sectors, bins),
            out_shape=jax.ShapeDtypeStruct((bins, 3, spheres), jnp.float32),
            in_specs=[vmem],
            out_specs=vmem,
            scratch_shapes=[
                pltpu.VMEM((sectors, bins, 3, spheres), jnp.float32),
                pltpu.VMEM((sectors, GHOSTS, 3, spheres), jnp.float32),
                pltpu.VMEM((sectors, GHOSTS, 3, spheres), jnp.float32),
                pltpu.SemaphoreType.DMA((3, sectors)),
                pltpu.SemaphoreType.DMA((3, sectors)),
            ],
            compiler_params=pltpu.CompilerParams(
                collective_id=1, has_side_effects=True, vmem_limit_bytes=32 * 2**20
            ),
        )(react)
        velocity_new, force_new = pl.pallas_call(
            finish_kernel,
            out_shape=(jax.ShapeDtypeStruct((bins, 3, spheres), jnp.float32),) * 2,
            in_specs=[vmem] * 3,
            out_specs=(hbm, hbm),
            scratch_shapes=[
                pltpu.VMEM((bins, 3, spheres), jnp.float32),
                pltpu.SemaphoreType.DMA((2,)),
            ],
        )(force, base, mass)
        return (moved, velocity_new, force_new)

    spec = P(("slab", "blk"))
    return jax.shard_map(
        local, mesh=mesh, in_specs=(spec,) * 6, out_specs=(spec,) * 3, check_vma=False
    )
```

profile of v0, /device:TPU:0, one launch (start us, length us, event | category | flops | bytes accessed | tf_op | source)
XLA Modules:
  0.0 56.8 jit_solution(9550715541675621466)
XLA Ops:
  0.6 0.8 %copy.12.neigh_in = s32[32,16]{1,0:T(8,128)S(1)} copy(s32[32,16]{0,1:T(8,128)} %param.10) | data formatting | bytes 4096 | tf_op args[4]
  1.4 0.0 copy-start.6
  1.4 0.8 %copy.9.pos_in = f32[32,3,128]{2,1,0:T(4,128)S(1)} copy(f32[32,3,128]{2,0,1:T(8,128)} %param.6) | data formatting | bytes 98304 | tf_op args[0]
  2.2 0.0 copy-done.6
  2.3 0.0 copy-start.7
  2.3 0.7 %copy-done.7 = f32[32,3,128]{2,0,1:T(8,128)S(1)} copy-done((f32[32,3,128]{2,0,1:T(8,128)S(1)}, f32[32,3,128]{2,0,1:T(8,128)}, u32[]{:S(2)}) %copy-start.7) | copy-done | bytes 49176
  3.1 0.0 copy-start.2
  3.1 0.0 copy-start.4
  3.1 0.7 %copy-done.2 = f32[32,128]{1,0:T(8,128)S(1)} copy-done((f32[32,128]{1,0:T(8,128)S(1)}, f32[32,128]{1,0:T(8,128)}, u32[]{:S(2)}) %copy-start.2) | copy-done | bytes 16408
  3.8 0.0 copy-done.4
  3.8 11.1 %shard_map.85 = (f32[4,48,4,128]{3,2,1,0:T(4,128)S(1)}, s32[4,32,16]{2,1,0:T(8,128)S(1)}, s32[4,1,32]{2,1,0:T(1,128)S(1)}, f32[32,3,128]{2,1,0:T(4,128)S(1)}, f32[32,1,128]{2,1,0:T(1,128)S(1)}) custom-call(f32[32,3,128]{2,1,0:T(4,128)S(1)} %copy.9.pos_in, f32[32,128]{1,0:T(8,128)S(1)} %copy-done.2, f32[32,3,128]{2,1,0:T(4,128)S(1)} %copy.10.vel_in, ...), custom_call_target="tpu_custom_call" | custom-call | tf_op jit(solution)/shard_map/pallas_call | solution.py:317
  14.9 0.0 copy-start.3
  14.9 0.6 %copy-done.3 = f32[32,1,128]{2,1,0:T(1,128)} copy-done((f32[32,1,128]{2,1,0:T(1,128)}, f32[32,1,128]{2,1,0:T(1,128)S(1)}, u32[]{:S(2)}) %copy-start.3) | copy-done | bytes 16408
  15.5 0.0 copy-start.1
  15.5 27.9 %shard_map.86 = (f32[32,3,128]{2,1,0:T(4,128)S(1)}, f32[4,48,3,128]{3,2,1,0:T(4,128)S(1)}) custom-call(s32[4,32,16]{2,1,0:T(8,128)S(1)} %get-tuple-element.12.neigh, s32[4,1,32]{2,1,0:T(1,128)S(1)} %get-tuple-element.13.count, f32[4,48,4,128]{3,2,1,0:T(4,128)S(1)} %get-tuple-element.14.ext), custom_call_target="tpu_custom_call" | custom-call | tf_op jit(solution)/shard_map/pallas_call | solution.py:341
  43.3 0.0 copy-done.1
  43.3 0.6 %copy.13 = f32[32,3,128]{2,0,1:T(8,128)} copy(f32[32,3,128]{2,1,0:T(4,128)S(1)} %get-tuple-element.21) | data formatting | bytes 98304
  44.0 8.5 %shard_map.87.force = f32[32,3,128]{2,1,0:T(4,128)S(1)} custom-call(f32[4,48,3,128]{3,2,1,0:T(4,128)S(1)} %get-tuple-element.16.react), custom_call_target="tpu_custom_call" | custom-call | tf_op jit(solution)/shard_map/pallas_call | solution.py:357
  52.5 0.0 copy-start
  52.5 0.6 %copy-done = f32[32,3,128]{2,1,0:T(4,128)} copy-done((f32[32,3,128]{2,1,0:T(4,128)}, f32[32,3,128]{2,1,0:T(4,128)S(1)}, u32[]{:S(2)}) %copy-start) | copy-done | bytes 49176
  53.1 1.6 %shard_map.88 = (f32[32,3,128]{2,1,0:T(4,128)}, f32[32,3,128]{2,1,0:T(4,128)}) custom-call(f32[32,3,128]{2,1,0:T(4,128)} %copy-done, f32[32,3,128]{2,1,0:T(4,128)} %copy-done.1, f32[32,1,128]{2,1,0:T(1,128)} %copy-done.3), custom_call_target="tpu_custom_call" | custom-call | tf_op jit(solution)/shard_map/pallas_call | solution.py:373
  54.7 0.0 copy-start.5
  54.7 1.5 %copy.14 = f32[32,3,128]{2,0,1:T(8,128)} copy(f32[32,3,128]{2,1,0:T(4,128)} %get-tuple-element.22) | data formatting | bytes 98304
  56.2 0.0 copy-done.5
  56.2 0.6 %copy.15 = f32[32,3,128]{2,0,1:T(8,128)} copy(f32[32,3,128]{2,1,0:T(4,128)S(1)} %copy-done.5) | data formatting | bytes 98304
  (2 shorter events, 0.1 us)
Async XLA Ops:
  1.4 0.8 %copy-start.6 = (f32[32,3,128]{2,0,1:T(8,128)S(1)}, f32[32,3,128]{2,0,1:T(8,128)}, u32[]{:S(2)}) copy-start(f32[32,3,128]{2,0,1:T(8,128)} %param.8) | copy-start | bytes 147460
  2.3 0.8 %copy-start.7 = (f32[32,3,128]{2,0,1:T(8,128)S(1)}, f32[32,3,128]{2,0,1:T(8,128)}, u32[]{:S(2)}) copy-start(f32[32,3,128]{2,0,1:T(8,128)} %param.9) | copy-start | bytes 147460
  3.1 0.7 %copy-start.2 = (f32[32,128]{1,0:T(8,128)S(1)}, f32[32,128]{1,0:T(8,128)}, u32[]{:S(2)}) copy-start(f32[32,128]{1,0:T(8,128)} %rad_in.1) | copy-start | bytes 49156
  3.1 0.7 %copy-start.4 = (s32[32]{0:T(128)S(1)}, s32[32]{0:T(128)}, u32[]{:S(2)}) copy-start(s32[32]{0:T(128)} %param.11) | copy-start | bytes 388
  14.9 0.6 %copy-start.3 = (f32[32,1,128]{2,1,0:T(1,128)}, f32[32,1,128]{2,1,0:T(1,128)S(1)}, u32[]{:S(2)}) copy-start(f32[32,1,128]{2,1,0:T(1,128)S(1)} %get-tuple-element.18.mass) | copy-start | bytes 49156
  15.5 27.9 %copy-start.1 = (f32[32,3,128]{2,1,0:T(4,128)}, f32[32,3,128]{2,1,0:T(4,128)S(1)}, u32[]{:S(2)}) copy-start(f32[32,3,128]{2,1,0:T(4,128)S(1)} %get-tuple-element.17.base) | copy-start | bytes 147460
  52.5 0.6 %copy-start = (f32[32,3,128]{2,1,0:T(4,128)}, f32[32,3,128]{2,1,0:T(4,128)S(1)}, u32[]{:S(2)}) copy-start(f32[32,3,128]{2,1,0:T(4,128)S(1)} %shard_map.87.force) | copy-start | bytes 147460
  54.7 1.5 %copy-start.5 = (f32[32,3,128]{2,1,0:T(4,128)S(1)}, f32[32,3,128]{2,1,0:T(4,128)}, u32[]{:S(2)}) copy-start(f32[32,3,128]{2,1,0:T(4,128)} %get-tuple-element.23) | copy-start | bytes 147460
where the time goes:
time: 57.7 us; the launch traced here: 56.8 us
  Pallas kernels  49 us (85%)
  local copies, waits for them, and re-layouts  7.09 us (12%)
  between operations  0.73 us (1%)
    pallas_call x1, Pallas kernels, local(): pl.pallas_call(functools.partial(tiles_kernel, sectors), out_shape=(jax.S...  27.9 us
    pallas_call x1, Pallas kernels, local(): pl.pallas_call(functools.partial(spread_kernel, slabs, sectors), out_shap...  11.1 us
    pallas_call x1, Pallas kernels, local(): pl.pallas_call(functools.partial(gather_kernel, slabs, sectors, bins), ou...  8.54 us
    unnamed x23, local copies, waits for them, and re-layouts  7.09 us
    pallas_call x1, Pallas kernels, local(): pl.pallas_call(finish_kernel, out_shape=(jax.ShapeDtypeStruct((bins, 3, s...  1.55 us

commit v1 on v0

--- a/solution.py
+++ b/solution.py
@@ -16,10 +16,9 @@
 MESH = pl.DeviceIdType.MESH
 
 
-def acceleration(force, radius):
-    accel = force / (125.0 * radius * radius * radius)
-    component = lax.broadcasted_iota(jnp.int32, accel.shape, 1)
-    return accel + jnp.where(component == 1, -0.5, 0.0)
+def acceleration(force, mass, component):
+    accel = force / mass
+    return accel - 0.5 if component == 1 else accel
 
 
 def greet(slabs, sectors):
@@ -50,7 +49,7 @@
     ext, neigh_all, count_all, base, mass, pos, rad, vel, old, send, recv, local,
 ):
     slab, sector = lax.axis_index("slab"), lax.axis_index("blk")
-    bins = pos.shape[0]
+    bins = pos.shape[1]
     fetches = [
         pltpu.make_async_copy(source, target, local.at[index])
         for index, (source, target) in enumerate((
@@ -63,11 +62,13 @@
     greet(slabs, sectors)
     for fetch in fetches:
         fetch.wait()
-    radius = rad[...][:, None, :]
-    accel_old = acceleration(old[...], radius)
-    moved = pos[...] + TIMESTEP * vel[...] + 0.5 * TIMESTEP * TIMESTEP * accel_old
-    ext[sector, pl.ds(GHOSTS, bins), 0:3, :] = moved
-    ext[sector, pl.ds(GHOSTS, bins), 3:4, :] = radius
+    radius = rad[...]
+    mass[...] = 125.0 * radius * radius * radius
+    accel_old = [acceleration(old[c], mass[...], c) for c in range(3)]
+    for c in range(3):
+        moved = pos[c] + TIMESTEP * vel[c] + 0.5 * TIMESTEP * TIMESTEP * accel_old[c]
+        ext[sector, pl.ds(GHOSTS, bins), c : c + 1, :] = moved[:, None, :]
+    ext[sector, pl.ds(GHOSTS, bins), 3:4, :] = radius[:, None, :]
 
     def mate(step, what):
         other = lax.rem(sector + step, sectors)
@@ -102,8 +103,8 @@
         for step in range(sectors):
             beside(step, 1).start()
 
-    base[...] = vel[...] + 0.5 * TIMESTEP * accel_old
-    mass[...] = 125.0 * radius * radius * radius
+    for c in range(3):
+        base[c] = vel[c] + 0.5 * TIMESTEP * accel_old[c]
     for step in range(1, sectors):
         for what in range(3):
             mate(step, what).wait()
@@ -121,22 +122,57 @@
             beside(step, 0).wait_recv()
 
 
-def tiles_kernel(sectors, neigh, count, ext, moved_out, react, acol, acc, moved, done):
+def tiles_kernel(sectors, neigh, count, ext, moved_out, react, acol, acc, select, moved, done):
     sector = lax.axis_index("blk")
-    bins = neigh.shape[1]
+    bins = neigh.shape[2]
     spheres = ext.shape[3]
     strips = spheres // 8
-    moved[...] = ext[sector, pl.ds(GHOSTS, bins), 0:3, :]
+    spare = bins + 2 * GHOSTS
+    for c in range(3):
+        moved[c] = ext[sector, pl.ds(GHOSTS, bins), c, :]
     store = pltpu.make_async_copy(moved, moved_out, done)
     store.start()
     react[...] = jnp.zeros_like(react)
     diagonal = lax.broadcasted_iota(jnp.int32, (spheres, spheres), 0) == lax.broadcasted_iota(
         jnp.int32, (spheres, spheres), 1
     )
+    piece = lax.broadcasted_iota(jnp.int32, select.shape, 0)
+    block = lax.broadcasted_iota(jnp.int32, select.shape, 1) // spheres
+    wanted = jnp.where(block == 4, 7, block)
+    select[...] = jnp.where(piece % 8 == wanted, 1.0, 0.0).astype(jnp.bfloat16)
+    ones = jnp.ones((2 * spheres, spheres), jnp.bfloat16)
+
+    def fill_columns(mine):
+        wide = jnp.concatenate([mine, 0.01 / mine[3:4], 0.01 / mine[3:4], 0.01 / mine[3:4], 0.01 / mine[3:4]], axis=0)
+        top = wide.astype(jnp.bfloat16).astype(jnp.float32)
+        middle = (wide - top).astype(jnp.bfloat16).astype(jnp.float32)
+        low = wide - top - middle
+        pieces = jnp.concatenate([top, middle, low, jnp.zeros_like(low)], axis=0).T
+        acol[...] = jnp.dot(
+            pieces.astype(jnp.bfloat16), select[...], preferred_element_type=jnp.float32
+        )
+
+    def row_sums():
+        whole = acc[...].reshape(3 * spheres, spheres)
+        top = whole.astype(jnp.bfloat16)
+        rest = (whole - top.astype(jnp.float32)).astype(jnp.bfloat16)
+        sums = jnp.dot(
+            jnp.concatenate([top, rest], axis=1), ones, preferred_element_type=jnp.float32
+        )
+        return jnp.concatenate(
+            [
+                jnp.sum(
+                    jnp.where(diagonal, sums[c * spheres : (c + 1) * spheres], 0.0),
+                    axis=0, keepdims=True,
+                )
+                for c in range(3)
+            ],
+            axis=0,
+        )
 
     def group_units(group):
         return lax.fori_loop(
-            0, bins, lambda own, t: t + count[group, 0, own] + BIN_COST, 0, unroll=bins
+            0, bins, lambda own, t: t + count[group, 0, own] + 1 + BIN_COST, 0, unroll=bins
         )
 
     sizes = [group_units(group) for group in range(sectors)]
@@ -144,7 +180,7 @@
     first = total * sector // sectors
     last = total * (sector + 1) // sectors
 
-    def pair(others, both):
+    def pair(others):
         rows_of = []
         for other in others:
             row = [jnp.broadcast_to(other[c : c + 1, :], (8, spheres)) for c in range(4)]
@@ -152,7 +188,7 @@
         totals = [[None] * 3 for _ in others]
         for strip in range(strips):
             rows = pl.ds(8 * strip, 8)
-            column = [acol[c, rows, :] for c in range(5)]
+            column = [acol[rows, c * spheres : (c + 1) * spheres] for c in range(5)]
             sums = [None] * 3
             for row, total_b in zip(rows_of, totals):
                 d = [column[c] - row[c] for c in range(3)]
@@ -165,64 +201,45 @@
                     w = pull * d[c]
                     total_b[c] = w if strip == 0 else total_b[c] + w
                     sums[c] = w if sums[c] is None else sums[c] + w
-            if both:
-                for c in range(3):
-                    acc[c, rows, :] += sums[c]
+            for c in range(3):
+                acc[c, rows, :] += sums[c]
         return [
             jnp.concatenate([jnp.sum(t, axis=0, keepdims=True) for t in total_b], axis=0)
             for total_b in totals
         ]
 
     def one_bin(group, own, start):
-        tiles = count[group, 0, own]
-        units = tiles + BIN_COST
+        tiles = count[group, 0, own] + 1
         low = jnp.maximum(first - start - BIN_COST, 0)
         high = jnp.minimum(last - start - BIN_COST, tiles)
-        alone = (start >= first) & (start < last)
-
-        @pl.when((high > low) | alone)
+
+        def unit(k):
+            other = neigh[group, jnp.maximum(k - 1, 0), own]
+            return jnp.where(k == 0, GHOSTS + own, other), jnp.where(k == 0, spare, other)
+
+        @pl.when(high > low)
         def _():
-            mine = ext[group, GHOSTS + own]
-            wide = jnp.concatenate([mine, 0.01 / mine], axis=0).T
-            for c, column in enumerate((0, 1, 2, 3, 7)):
-                acol[c] = jnp.broadcast_to(wide[:, column : column + 1], (spheres, spheres))
-
-            @pl.when(alone)
+            fill_columns(ext[group, GHOSTS + own])
+            acc[...] = jnp.zeros_like(acc)
+            twos = (high - low) // 2
+
+            def two_tiles(k, _):
+                (one, to_one), (two, to_two) = unit(low + 2 * k), unit(low + 2 * k + 1)
+                forces = pair([ext[group, one], ext[group, two]])
+                react[group, to_one] -= forces[0]
+                react[group, to_two] -= forces[1]
+                return 0
+
+            lax.fori_loop(0, twos, two_tiles, 0)
+
+            @pl.when(low + 2 * twos < high)
             def _():
-                react[group, GHOSTS + own] -= pair([mine], False)[0]
-
-            @pl.when(high > low)
-            def _():
-                acc[...] = jnp.zeros_like(acc)
-                twos = (high - low) // 2
-
-                def two_tiles(k, _):
-                    one = neigh[group, own, low + 2 * k]
-                    two = neigh[group, own, low + 2 * k + 1]
-                    forces = pair([ext[group, one], ext[group, two]], True)
-                    react[group, one] -= forces[0]
-                    react[group, two] -= forces[1]
-                    return 0
-
-                lax.fori_loop(0, twos, two_tiles, 0)
-
-                @pl.when(low + 2 * twos < high)
-                def _():
-                    one = neigh[group, own, high - 1]
-                    react[group, one] -= pair([ext[group, one]], True)[0]
-
-                react[group, GHOSTS + own] += jnp.concatenate(
-                    [
-                        jnp.sum(
-                            jnp.where(diagonal, jnp.sum(acc[c], axis=1, keepdims=True), 0.0),
-                            axis=0, keepdims=True,
-                        )
-                        for c in range(3)
-                    ],
-                    axis=0,
-                )
-
-        return start + units
+                one, to_one = unit(high - 1)
+                react[group, to_one] -= pair([ext[group, one]])[0]
+
+            react[group, GHOSTS + own] += row_sums()
+
+        return start + tiles + BIN_COST
 
     def one_group(group, start):
         stop = start
@@ -292,12 +309,13 @@
             total[pl.ds(bins - GHOSTS, GHOSTS)] += above[step]
 
 
-def finish_kernel(force, base, mass, velocity_out, force_out, velocity, done):
-    copy_force = pltpu.make_async_copy(force, force_out, done.at[0])
+def finish_kernel(force, base, mass, velocity_out, force_out, velocity, turned, done):
+    for c in range(3):
+        turned[c] = force[:, c, :]
+    copy_force = pltpu.make_async_copy(turned, force_out, done.at[0])
     copy_force.start()
-    component = lax.broadcasted_iota(jnp.int32, force.shape, 1)
-    accel = force[...] / mass[...] + jnp.where(component == 1, -0.5, 0.0)
-    velocity[...] = base[...] + 0.5 * TIMESTEP * accel
+    for c in range(3):
+        velocity[c] = base[c] + 0.5 * TIMESTEP * acceleration(turned[c], mass[...], c)
     copy_velocity = pltpu.make_async_copy(velocity, velocity_out, done.at[1])
     copy_velocity.start()
     copy_force.wait()
@@ -312,47 +330,52 @@
 
     def local(positions, radius, velocity, old_force, neighbours, tile_count):
         bins, _, spheres = positions.shape
+        first_axis = lambda array: jnp.transpose(array, (1, 0, 2))
         slots = neighbours.shape[1]
         candidates = bins + 2 * GHOSTS
         ext, neigh_all, count_all, base, mass = pl.pallas_call(
             functools.partial(spread_kernel, slabs, sectors),
             out_shape=(
                 jax.ShapeDtypeStruct((sectors, candidates, 4, spheres), jnp.float32),
-                jax.ShapeDtypeStruct((sectors, bins, slots), jnp.int32),
+                jax.ShapeDtypeStruct((sectors, slots, bins), jnp.int32),
                 jax.ShapeDtypeStruct((sectors, 1, bins), jnp.int32),
-                jax.ShapeDtypeStruct((bins, 3, spheres), jnp.float32),
-                jax.ShapeDtypeStruct((bins, 1, spheres), jnp.float32),
+                jax.ShapeDtypeStruct((3, bins, spheres), jnp.float32),
+                jax.ShapeDtypeStruct((bins, spheres), jnp.float32),
             ),
             in_specs=[hbm] * 6,
             out_specs=(vmem,) * 5,
             scratch_shapes=[
-                pltpu.VMEM((bins, 3, spheres), jnp.float32),
+                pltpu.VMEM((3, bins, spheres), jnp.float32),
                 pltpu.VMEM((bins, spheres), jnp.float32),
-                pltpu.VMEM((bins, 3, spheres), jnp.float32),
-                pltpu.VMEM((bins, 3, spheres), jnp.float32),
+                pltpu.VMEM((3, bins, spheres), jnp.float32),
+                pltpu.VMEM((3, bins, spheres), jnp.float32),
                 pltpu.SemaphoreType.DMA((5, sectors)),
                 pltpu.SemaphoreType.DMA((5, sectors)),
                 pltpu.SemaphoreType.DMA((6,)),
             ],
             compiler_params=pltpu.CompilerParams(
-                collective_id=0, has_side_effects=True, vmem_limit_bytes=32 * 2**20
+                collective_id=0, has_side_effects=True, vmem_limit_bytes=8 * 2**20
             ),
-        )(positions, radius, velocity, old_force, neighbours, tile_count.reshape(1, bins))
+        )(
+            first_axis(positions), radius, first_axis(velocity), first_axis(old_force),
+            neighbours.T, tile_count.reshape(1, bins),
+        )
         moved, react = pl.pallas_call(
             functools.partial(tiles_kernel, sectors),
             out_shape=(
-                jax.ShapeDtypeStruct((bins, 3, spheres), jnp.float32),
-                jax.ShapeDtypeStruct((sectors, candidates, 3, spheres), jnp.float32),
+                jax.ShapeDtypeStruct((3, bins, spheres), jnp.float32),
+                jax.ShapeDtypeStruct((sectors, candidates + 1, 3, spheres), jnp.float32),
             ),
             in_specs=[smem, smem, vmem],
             out_specs=(hbm, vmem),
             scratch_shapes=[
-                pltpu.VMEM((5, spheres, spheres), jnp.float32),
+                pltpu.VMEM((spheres, 5 * spheres), jnp.float32),
                 pltpu.VMEM((3, spheres, spheres), jnp.float32),
-                pltpu.VMEM((bins, 3, spheres), jnp.float32),
+                pltpu.VMEM((32, 5 * spheres), jnp.bfloat16),
+                pltpu.VMEM((3, bins, spheres), jnp.float32),
                 pltpu.SemaphoreType.DMA,
             ],
-            compiler_params=pltpu.CompilerParams(vmem_limit_bytes=32 * 2**20),
+            compiler_params=pltpu.CompilerParams(vmem_limit_bytes=8 * 2**20),
         )(neigh_all, count_all, ext)
         force = pl.pallas_call(
             functools.partial(gather_kernel, slabs, sectors, bins),
@@ -367,20 +390,22 @@
                 pltpu.SemaphoreType.DMA((3, sectors)),
             ],
             compiler_params=pltpu.CompilerParams(
-                collective_id=1, has_side_effects=True, vmem_limit_bytes=32 * 2**20
+                collective_id=1, has_side_effects=True, vmem_limit_bytes=8 * 2**20
             ),
         )(react)
         velocity_new, force_new = pl.pallas_call(
             finish_kernel,
-            out_shape=(jax.ShapeDtypeStruct((bins, 3, spheres), jnp.float32),) * 2,
+            out_shape=(jax.ShapeDtypeStruct((3, bins, spheres), jnp.float32),) * 2,
             in_specs=[vmem] * 3,
             out_specs=(hbm, hbm),
             scratch_shapes=[
-                pltpu.VMEM((bins, 3, spheres), jnp.float32),
+                pltpu.VMEM((3, bins, spheres), jnp.float32),
+                pltpu.VMEM((3, bins, spheres), jnp.float32),
                 pltpu.SemaphoreType.DMA((2,)),
             ],
+            compiler_params=pltpu.CompilerParams(vmem_limit_bytes=8 * 2**20),
         )(force, base, mass)
-        return (moved, velocity_new, force_new)
+        return (first_axis(moved), first_axis(velocity_new), first_axis(force_new))
 
     spec = P(("slab", "blk"))
     return jax.shard_map(

time: 57.7 us -> 55.5 us (0.962)
  local copies, waits for them, and re-layouts: 7.09 us -> 3.8 us
  Pallas kernels: 49 us -> 50.4 us
    unnamed x23 -> x12, local copies, waits for them, and re-layouts: 7.09 us -> 3.8 us
    pallas_call x1, Pallas kernels: 27.9 us -> 30.4 us  [local(): pl.pallas_call(functools.partial(tiles_kernel, sectors), out_shape=(jax.S...]
    pallas_call x1, Pallas kernels: 1.55 us -> 0.69 us  [local(): pl.pallas_call(finish_kernel, out_shape=(jax.ShapeDtypeStruct((3, bins, s...]
where the time goes in v1:
time: 55.5 us; the launch traced here: 54.9 us
  Pallas kernels  50.4 us (91%)
  local copies, waits for them, and re-layouts  3.8 us (7%)
  between operations  0.68 us (1%)
    pallas_call x1, Pallas kernels, local(): pl.pallas_call(functools.partial(tiles_kernel, sectors), out_shape=(jax.S...  30.4 us
    pallas_call x1, Pallas kernels, local(): pl.pallas_call(functools.partial(spread_kernel, slabs, sectors), out_shap...  10.8 us
    pallas_call x1, Pallas kernels, local(): pl.pallas_call(functools.partial(gather_kernel, slabs, sectors, bins), ou...  8.47 us
    unnamed x12, local copies, waits for them, and re-layouts  3.8 us

profile of v1, /device:TPU:0, one launch (start us, length us, event | category | flops | bytes accessed | tf_op | source)
XLA Modules:
  0.0 54.9 jit_solution(104777396527231638)
XLA Ops:
  0.6 0.0 copy-start.4
  0.6 0.0 copy-start.5
  0.7 0.7 %copy-done.4 = s32[32,16]{0,1:T(8,128)S(1)} copy-done((s32[32,16]{0,1:T(8,128)S(1)}, s32[32,16]{0,1:T(8,128)}, u32[]{:S(2)}) %copy-start.4) | copy-done | bytes 2072
  1.3 0.0 copy-done.5
  1.3 0.0 copy-start
  1.3 0.8 %copy-done = f32[32,3,128]{2,0,1:T(8,128)S(1)} copy-done((f32[32,3,128]{2,0,1:T(8,128)S(1)}, f32[32,3,128]{2,0,1:T(8,128)}, u32[]{:S(2)}) %copy-start) | copy-done | bytes 49176
  2.1 0.0 copy-start.1
  2.1 0.8 %copy-done.1 = f32[32,3,128]{2,0,1:T(8,128)S(1)} copy-done((f32[32,3,128]{2,0,1:T(8,128)S(1)}, f32[32,3,128]{2,0,1:T(8,128)}, u32[]{:S(2)}) %copy-start.1) | copy-done | bytes 49176
  2.9 0.0 copy-start.2
  2.9 0.8 %copy-done.2 = f32[32,3,128]{2,0,1:T(8,128)S(1)} copy-done((f32[32,3,128]{2,0,1:T(8,128)S(1)}, f32[32,3,128]{2,0,1:T(8,128)}, u32[]{:S(2)}) %copy-start.2) | copy-done | bytes 49176
  3.7 0.0 copy-start.3
  3.7 0.7 %copy-done.3 = f32[32,128]{1,0:T(8,128)S(1)} copy-done((f32[32,128]{1,0:T(8,128)S(1)}, f32[32,128]{1,0:T(8,128)}, u32[]{:S(2)}) %copy-start.3) | copy-done | bytes 16408
  4.4 10.8 %shard_map.85 = (f32[4,48,4,128]{3,2,1,0:T(4,128)S(1)}, s32[4,16,32]{2,1,0:T(8,128)S(1)}, s32[4,1,32]{2,1,0:T(1,128)S(1)}, f32[3,32,128]{2,1,0:T(8,128)S(1)}, f32[32,128]{1,0:T(8,128)S(1)}) custom-call(f32[3,32,128]{2,1,0:T(8,128)S(1)} %bitcast.8, f32[32,128]{1,0:T(8,128)S(1)} %copy-done.3, f32[3,32,128]{2,1,0:T(8,128)S(1)} %bitcast.9, ...), custom_call_target="tpu_custom_call" | custom-call | tf_op jit(solution)/shard_map/pallas_call | solution.py:336
  15.3 30.4 %shard_map.86 = (f32[3,32,128]{2,1,0:T(8,128)}, f32[4,49,3,128]{3,2,1,0:T(4,128)S(1)}) custom-call(s32[4,16,32]{2,1,0:T(8,128)S(1)} %get-tuple-element.12.neigh, s32[4,1,32]{2,1,0:T(1,128)S(1)} %get-tuple-element.13.count, f32[4,48,4,128]{3,2,1,0:T(4,128)S(1)} %get-tuple-element.14.ext), custom_call_target="tpu_custom_call" | custom-call | tf_op jit(solution)/shard_map/pallas_call | solution.py:363
  45.7 8.5 %shard_map.87.force = f32[32,3,128]{2,1,0:T(4,128)S(1)} custom-call(f32[4,49,3,128]{3,2,1,0:T(4,128)S(1)} %get-tuple-element.16.react), custom_call_target="tpu_custom_call" | custom-call | tf_op jit(solution)/shard_map/pallas_call | solution.py:380
  54.2 0.7 %shard_map.88 = (f32[3,32,128]{2,1,0:T(8,128)}, f32[3,32,128]{2,1,0:T(8,128)}) custom-call(f32[32,3,128]{2,1,0:T(4,128)S(1)} %shard_map.87.force, f32[3,32,128]{2,1,0:T(8,128)S(1)} %get-tuple-element.17.base, f32[32,128]{1,0:T(8,128)S(1)} %get-tuple-element.18.mass), custom_call_target="tpu_custom_call" | custom-call | tf_op jit(solution)/shard_map/pallas_call | solution.py:396
Async XLA Ops:
  0.6 0.7 %copy-start.4 = (s32[32,16]{0,1:T(8,128)S(1)}, s32[32,16]{0,1:T(8,128)}, u32[]{:S(2)}) copy-start(s32[32,16]{0,1:T(8,128)} %param.10) | copy-start | bytes 6148
  0.6 0.7 %copy-start.5 = (s32[32]{0:T(128)S(1)}, s32[32]{0:T(128)}, u32[]{:S(2)}) copy-start(s32[32]{0:T(128)} %param.11) | copy-start | bytes 388
  1.3 0.8 %copy-start = (f32[32,3,128]{2,0,1:T(8,128)S(1)}, f32[32,3,128]{2,0,1:T(8,128)}, u32[]{:S(2)}) copy-start(f32[32,3,128]{2,0,1:T(8,128)} %param.6) | copy-start | bytes 147460
  2.1 0.8 %copy-start.1 = (f32[32,3,128]{2,0,1:T(8,128)S(1)}, f32[32,3,128]{2,0,1:T(8,128)}, u32[]{:S(2)}) copy-start(f32[32,3,128]{2,0,1:T(8,128)} %param.8) | copy-start | bytes 147460
  2.9 0.8 %copy-start.2 = (f32[32,3,128]{2,0,1:T(8,128)S(1)}, f32[32,3,128]{2,0,1:T(8,128)}, u32[]{:S(2)}) copy-start(f32[32,3,128]{2,0,1:T(8,128)} %param.9) | copy-start | bytes 147460
  3.7 0.7 %copy-start.3 = (f32[32,128]{1,0:T(8,128)S(1)}, f32[32,128]{1,0:T(8,128)}, u32[]{:S(2)}) copy-start(f32[32,128]{1,0:T(8,128)} %rad_in.1) | copy-start | bytes 49156

commit v2 on v1

--- a/solution.py
+++ b/solution.py
@@ -13,6 +13,7 @@
 TIMESTEP = 0.2
 TINY = 1e-30
 BIN_COST = 3
+CHUNK = 4
 MESH = pl.DeviceIdType.MESH
 
 
@@ -122,7 +123,7 @@
             beside(step, 0).wait_recv()
 
 
-def tiles_kernel(sectors, neigh, count, ext, moved_out, react, acol, acc, select, moved, done):
+def tiles_kernel(sectors, neigh, count, ext, moved_out, react, acol, acc, moved, done):
     sector = lax.axis_index("blk")
     bins = neigh.shape[2]
     spheres = ext.shape[3]
@@ -136,33 +137,18 @@
     diagonal = lax.broadcasted_iota(jnp.int32, (spheres, spheres), 0) == lax.broadcasted_iota(
         jnp.int32, (spheres, spheres), 1
     )
-    piece = lax.broadcasted_iota(jnp.int32, select.shape, 0)
-    block = lax.broadcasted_iota(jnp.int32, select.shape, 1) // spheres
-    wanted = jnp.where(block == 4, 7, block)
-    select[...] = jnp.where(piece % 8 == wanted, 1.0, 0.0).astype(jnp.bfloat16)
-    ones = jnp.ones((2 * spheres, spheres), jnp.bfloat16)
-
-    def fill_columns(mine):
-        wide = jnp.concatenate([mine, 0.01 / mine[3:4], 0.01 / mine[3:4], 0.01 / mine[3:4], 0.01 / mine[3:4]], axis=0)
-        top = wide.astype(jnp.bfloat16).astype(jnp.float32)
-        middle = (wide - top).astype(jnp.bfloat16).astype(jnp.float32)
-        low = wide - top - middle
-        pieces = jnp.concatenate([top, middle, low, jnp.zeros_like(low)], axis=0).T
-        acol[...] = jnp.dot(
-            pieces.astype(jnp.bfloat16), select[...], preferred_element_type=jnp.float32
-        )
-
-    def row_sums():
-        whole = acc[...].reshape(3 * spheres, spheres)
-        top = whole.astype(jnp.bfloat16)
-        rest = (whole - top.astype(jnp.float32)).astype(jnp.bfloat16)
-        sums = jnp.dot(
-            jnp.concatenate([top, rest], axis=1), ones, preferred_element_type=jnp.float32
-        )
+
+    def fill_columns(slot, mine):
+        wide = jnp.concatenate([mine, 0.01 / mine], axis=0).T
+        for c, column in enumerate((0, 1, 2, 3, 7)):
+            acol[slot, c] = jnp.broadcast_to(wide[:, column : column + 1], (spheres, spheres))
+        acc[slot] = jnp.zeros((3, spheres, spheres), jnp.float32)
+
+    def row_sums(slot):
         return jnp.concatenate(
             [
                 jnp.sum(
-                    jnp.where(diagonal, sums[c * spheres : (c + 1) * spheres], 0.0),
+                    jnp.where(diagonal, jnp.sum(acc[slot, c], axis=1, keepdims=True), 0.0),
                     axis=0, keepdims=True,
                 )
                 for c in range(3)
@@ -180,7 +166,7 @@
     first = total * sector // sectors
     last = total * (sector + 1) // sectors
 
-    def pair(others):
+    def pair(slot, others):
         rows_of = []
         for other in others:
             row = [jnp.broadcast_to(other[c : c + 1, :], (8, spheres)) for c in range(4)]
@@ -188,7 +174,7 @@
         totals = [[None] * 3 for _ in others]
         for strip in range(strips):
             rows = pl.ds(8 * strip, 8)
-            column = [acol[rows, c * spheres : (c + 1) * spheres] for c in range(5)]
+            column = [acol[slot, c, rows, :] for c in range(5)]
             sums = [None] * 3
             for row, total_b in zip(rows_of, totals):
                 d = [column[c] - row[c] for c in range(3)]
@@ -202,44 +188,56 @@
                     total_b[c] = w if strip == 0 else total_b[c] + w
                     sums[c] = w if sums[c] is None else sums[c] + w
             for c in range(3):
-                acc[c, rows, :] += sums[c]
+                acc[slot, c, rows, :] += sums[c]
         return [
             jnp.concatenate([jnp.sum(t, axis=0, keepdims=True) for t in total_b], axis=0)
             for total_b in totals
         ]
 
-    def one_bin(group, own, start):
+    def one_bin(group, chunk, slot, start):
+        own = chunk * CHUNK + slot
         tiles = count[group, 0, own] + 1
         low = jnp.maximum(first - start - BIN_COST, 0)
-        high = jnp.minimum(last - start - BIN_COST, tiles)
+        high = jnp.maximum(jnp.minimum(last - start - BIN_COST, tiles), low)
 
         def unit(k):
             other = neigh[group, jnp.maximum(k - 1, 0), own]
             return jnp.where(k == 0, GHOSTS + own, other), jnp.where(k == 0, spare, other)
 
-        @pl.when(high > low)
+        twos = (high - low) // 2
+
+        def two_tiles(k, _):
+            (one, to_one), (two, to_two) = unit(low + 2 * k), unit(low + 2 * k + 1)
+            forces = pair(slot, [ext[group, one], ext[group, two]])
+            react[group, to_one] -= forces[0]
+            react[group, to_two] -= forces[1]
+            return 0
+
+        lax.fori_loop(0, twos, two_tiles, 0)
+
+        @pl.when(low + 2 * twos < high)
         def _():
-            fill_columns(ext[group, GHOSTS + own])
-            acc[...] = jnp.zeros_like(acc)
-            twos = (high - low) // 2
-
-            def two_tiles(k, _):
-                (one, to_one), (two, to_two) = unit(low + 2 * k), unit(low + 2 * k + 1)
-                forces = pair([ext[group, one], ext[group, two]])
-                react[group, to_one] -= forces[0]
-                react[group, to_two] -= forces[1]
-                return 0
-
-            lax.fori_loop(0, twos, two_tiles, 0)
-
-            @pl.when(low + 2 * twos < high)
-            def _():
-                one, to_one = unit(high - 1)
-                react[group, to_one] -= pair([ext[group, one]])[0]
-
-            react[group, GHOSTS + own] += row_sums()
+            one, to_one = unit(high - 1)
+            react[group, to_one] -= pair(slot, [ext[group, one]])[0]
 
         return start + tiles + BIN_COST
+
+    def one_chunk(group, chunk, start):
+        stop = start
+        for slot in range(CHUNK):
+            stop += count[group, 0, chunk * CHUNK + slot] + 1 + BIN_COST
+
+        @pl.when((stop > first) & (start < last))
+        def _():
+            here = GHOSTS + chunk * CHUNK
+            for slot in range(CHUNK):
+                fill_columns(slot, ext[group, here + slot])
+            lax.fori_loop(0, CHUNK, functools.partial(one_bin, group, chunk), start)
+            sums = [row_sums(slot) for slot in range(CHUNK)]
+            for slot in range(CHUNK):
+                react[group, here + slot] += sums[slot]
+
+        return stop
 
     def one_group(group, start):
         stop = start
@@ -247,7 +245,7 @@
             stop += jnp.where(group == other, sizes[other], 0)
         touched = (stop > first) & (start < last)
         lax.fori_loop(
-            0, jnp.where(touched, bins, 0), functools.partial(one_bin, group), start
+            0, jnp.where(touched, bins // CHUNK, 0), functools.partial(one_chunk, group), start
         )
         return stop
 
@@ -354,7 +352,7 @@
                 pltpu.SemaphoreType.DMA((6,)),
             ],
             compiler_params=pltpu.CompilerParams(
-                collective_id=0, has_side_effects=True, vmem_limit_bytes=8 * 2**20
+                collective_id=0, has_side_effects=True, vmem_limit_bytes=60 * 2**20
             ),
         )(
             first_axis(positions), radius, first_axis(velocity), first_axis(old_force),
@@ -369,9 +367,8 @@
             in_specs=[smem, smem, vmem],
             out_specs=(hbm, vmem),
             scratch_shapes=[
-                pltpu.VMEM((spheres, 5 * spheres), jnp.float32),
-                pltpu.VMEM((3, spheres, spheres), jnp.float32),
-                pltpu.VMEM((32, 5 * spheres), jnp.bfloat16),
+                pltpu.VMEM((CHUNK, 5, spheres, spheres), jnp.float32),
+                pltpu.VMEM((CHUNK, 3, spheres, spheres), jnp.float32),
                 pltpu.VMEM((3, bins, spheres), jnp.float32),
                 pltpu.SemaphoreType.DMA,
             ],

time: 55.5 us -> 45.4 us (0.82)
  Pallas kernels: 50.4 us -> 42.1 us
  local copies, waits for them, and re-layouts: 3.8 us -> 2.42 us
    pallas_call x1, Pallas kernels: 30.4 us -> 21.4 us  [local(): pl.pallas_call(functools.partial(tiles_kernel, sectors), out_shape=(jax.S...]
    unnamed x12 -> x10, local copies, waits for them, and re-layouts: 3.8 us -> 2.42 us
    pallas_call x1, Pallas kernels: 10.8 us -> 11.4 us  [local(): pl.pallas_call(functools.partial(spread_kernel, slabs, sectors), out_shap...]
where the time goes in v2:
time: 45.4 us; the launch traced here: 45.3 us
  Pallas kernels  42.1 us (93%)
  local copies, waits for them, and re-layouts  2.42 us (5%)
  between operations  0.7 us (2%)
    pallas_call x1, Pallas kernels, local(): pl.pallas_call(functools.partial(tiles_kernel, sectors), out_shape=(jax.S...  21.4 us
    pallas_call x1, Pallas kernels, local(): pl.pallas_call(functools.partial(spread_kernel, slabs, sectors), out_shap...  11.4 us
    pallas_call x1, Pallas kernels, local(): pl.pallas_call(functools.partial(gather_kernel, slabs, sectors, bins), ou...  8.68 us
    unnamed x10, local copies, waits for them, and re-layouts  2.42 us

profile of v2, /device:TPU:0, one launch (start us, length us, event | category | flops | bytes accessed | tf_op | source)
XLA Modules:
  0.0 45.3 jit_solution(1103138476311353087)
XLA Ops:
  0.6 11.4 %shard_map.85 = (f32[4,48,4,128]{3,2,1,0:T(4,128)}, s32[4,16,32]{2,1,0:T(8,128)}, s32[4,1,32]{2,1,0:T(1,128)}, f32[3,32,128]{2,1,0:T(8,128)}, f32[32,128]{1,0:T(8,128)}) custom-call(f32[3,32,128]{2,1,0:T(8,128)} %bitcast.8, f32[32,128]{1,0:T(8,128)} %rad_in.1, f32[3,32,128]{2,1,0:T(8,128)} %bitcast.9, f32[3,32,128]{2,1,0:T(8,128)} %bitcast.10, ...), custom_call_target="tpu_custom_call" | custom-call | tf_op jit(solution)/shard_map/pallas_call | solution.py:334
  12.1 0.0 copy-start.4
  12.1 0.7 %copy-done.4 = s32[4,1,32]{2,1,0:T(1,128)S(1)} copy-done((s32[4,1,32]{2,1,0:T(1,128)S(1)}, s32[4,1,32]{2,1,0:T(1,128)}, u32[]{:S(2)}) %copy-start.4) | copy-done | bytes 536
  12.7 0.0 copy-start
  12.7 1.0 %copy-done = f32[4,48,4,128]{3,2,1,0:T(4,128)S(1)} copy-done((f32[4,48,4,128]{3,2,1,0:T(4,128)S(1)}, f32[4,48,4,128]{3,2,1,0:T(4,128)}, u32[]{:S(2)}) %copy-start) | copy-done | bytes 393240
  13.7 0.0 copy-start.2
  13.7 0.8 %copy-done.2 = s32[4,16,32]{2,1,0:T(8,128)S(1)} copy-done((s32[4,16,32]{2,1,0:T(8,128)S(1)}, s32[4,16,32]{2,1,0:T(8,128)}, u32[]{:S(2)}) %copy-start.2) | copy-done | bytes 8216
  14.5 21.4 %shard_map.86 = (f32[3,32,128]{2,1,0:T(8,128)}, f32[4,49,3,128]{3,2,1,0:T(4,128)S(1)}) custom-call(s32[4,16,32]{2,1,0:T(8,128)S(1)} %copy-done.2, s32[4,1,32]{2,1,0:T(1,128)S(1)} %copy-done.4, f32[4,48,4,128]{3,2,1,0:T(4,128)S(1)} %copy-done), custom_call_target="tpu_custom_call" | custom-call | tf_op jit(solution)/shard_map/pallas_call | solution.py:361
  35.9 0.0 copy-start.1
  35.9 0.0 copy-start.3
  35.9 8.7 %shard_map.87.force = f32[32,3,128]{2,1,0:T(4,128)S(1)} custom-call(f32[4,49,3,128]{3,2,1,0:T(4,128)S(1)} %get-tuple-element.16.react), custom_call_target="tpu_custom_call" | custom-call | tf_op jit(solution)/shard_map/pallas_call | solution.py:377
  44.6 0.0 copy-done.1
  44.6 0.0 copy-done.3
  44.6 0.7 %shard_map.88 = (f32[3,32,128]{2,1,0:T(8,128)}, f32[3,32,128]{2,1,0:T(8,128)}) custom-call(f32[32,3,128]{2,1,0:T(4,128)S(1)} %shard_map.87.force, f32[3,32,128]{2,1,0:T(8,128)S(1)} %copy-done.1, f32[32,128]{1,0:T(8,128)S(1)} %copy-done.3), custom_call_target="tpu_custom_call" | custom-call | tf_op jit(solution)/shard_map/pallas_call | solution.py:393
Async XLA Ops:
  12.1 0.7 %copy-start.4 = (s32[4,1,32]{2,1,0:T(1,128)S(1)}, s32[4,1,32]{2,1,0:T(1,128)}, u32[]{:S(2)}) copy-start(s32[4,1,32]{2,1,0:T(1,128)} %get-tuple-element.13.count) | copy-start | bytes 1540
  12.7 1.0 %copy-start = (f32[4,48,4,128]{3,2,1,0:T(4,128)S(1)}, f32[4,48,4,128]{3,2,1,0:T(4,128)}, u32[]{:S(2)}) copy-start(f32[4,48,4,128]{3,2,1,0:T(4,128)} %get-tuple-element.14.ext) | copy-start | bytes 1179652
  13.7 0.8 %copy-start.2 = (s32[4,16,32]{2,1,0:T(8,128)S(1)}, s32[4,16,32]{2,1,0:T(8,128)}, u32[]{:S(2)}) copy-start(s32[4,16,32]{2,1,0:T(8,128)} %get-tuple-element.12.neigh) | copy-start | bytes 24580
  35.9 8.7 %copy-start.1 = (f32[3,32,128]{2,1,0:T(8,128)S(1)}, f32[3,32,128]{2,1,0:T(8,128)}, u32[]{:S(2)}) copy-start(f32[3,32,128]{2,1,0:T(8,128)} %get-tuple-element.17.base) | copy-start | bytes 147460
  35.9 8.7 %copy-start.3 = (f32[32,128]{1,0:T(8,128)S(1)}, f32[32,128]{1,0:T(8,128)}, u32[]{:S(2)}) copy-start(f32[32,128]{1,0:T(8,128)} %get-tuple-element.18.mass) | copy-start | bytes 49156

commit v3 on v2

--- a/solution.py
+++ b/solution.py
@@ -12,7 +12,7 @@
 SOFTENING = 0.0025
 TIMESTEP = 0.2
 TINY = 1e-30
-BIN_COST = 3
+BIN_COST = 2
 CHUNK = 4
 MESH = pl.DeviceIdType.MESH
 
@@ -123,7 +123,7 @@
             beside(step, 0).wait_recv()
 
 
-def tiles_kernel(sectors, neigh, count, ext, moved_out, react, acol, acc, moved, done):
+def tiles_kernel(sectors, neigh, count, ext, moved_out, react, acol, acc_one, acc_two, items, moved, done):
     sector = lax.axis_index("blk")
     bins = neigh.shape[2]
     spheres = ext.shape[3]
@@ -142,13 +142,14 @@
         wide = jnp.concatenate([mine, 0.01 / mine], axis=0).T
         for c, column in enumerate((0, 1, 2, 3, 7)):
             acol[slot, c] = jnp.broadcast_to(wide[:, column : column + 1], (spheres, spheres))
-        acc[slot] = jnp.zeros((3, spheres, spheres), jnp.float32)
+        for acc in (acc_one, acc_two):
+            acc[slot] = jnp.zeros((3, spheres, spheres), jnp.float32)
 
     def row_sums(slot):
         return jnp.concatenate(
             [
                 jnp.sum(
-                    jnp.where(diagonal, jnp.sum(acc[slot, c], axis=1, keepdims=True), 0.0),
+                    jnp.where(diagonal, jnp.sum(acc_one[slot, c] + acc_two[slot, c], axis=1, keepdims=True), 0.0),
                     axis=0, keepdims=True,
                 )
                 for c in range(3)
@@ -166,17 +167,18 @@
     first = total * sector // sectors
     last = total * (sector + 1) // sectors
 
-    def pair(slot, others):
+    def run(group, first_item, how_many):
+        places = [[items[row, first_item + step] for row in range(3)] for step in range(how_many)]
         rows_of = []
-        for other in others:
-            row = [jnp.broadcast_to(other[c : c + 1, :], (8, spheres)) for c in range(4)]
+        for _, other, _ in places:
+            values = ext[group, other]
+            row = [jnp.broadcast_to(values[c : c + 1, :], (8, spheres)) for c in range(4)]
             rows_of.append(row + [0.01 / row[3]])
-        totals = [[None] * 3 for _ in others]
+        totals = [[None] * 3 for _ in places]
         for strip in range(strips):
             rows = pl.ds(8 * strip, 8)
-            column = [acol[slot, c, rows, :] for c in range(5)]
-            sums = [None] * 3
-            for row, total_b in zip(rows_of, totals):
+            for (slot, _, _), row, total_b, acc in zip(places, rows_of, totals, (acc_one, acc_two)):
+                column = [acol[slot, c, rows, :] for c in range(5)]
                 d = [column[c] - row[c] for c in range(3)]
                 square = d[0] * d[0] + d[1] * d[1] + (d[2] * d[2] + SOFTENING)
                 inverse = lax.rsqrt(square)
@@ -186,41 +188,36 @@
                 for c in range(3):
                     w = pull * d[c]
                     total_b[c] = w if strip == 0 else total_b[c] + w
-                    sums[c] = w if sums[c] is None else sums[c] + w
-            for c in range(3):
-                acc[slot, c, rows, :] += sums[c]
-        return [
+                    acc[slot, c, rows, :] += w
+        sums = [
             jnp.concatenate([jnp.sum(t, axis=0, keepdims=True) for t in total_b], axis=0)
             for total_b in totals
         ]
-
-    def one_bin(group, chunk, slot, start):
+        for (_, _, place), force in zip(places, sums):
+            react[group, place] -= force
+
+    def note_bin(group, chunk, slot, carry):
+        start, size = carry
         own = chunk * CHUNK + slot
         tiles = count[group, 0, own] + 1
         low = jnp.maximum(first - start - BIN_COST, 0)
         high = jnp.maximum(jnp.minimum(last - start - BIN_COST, tiles), low)
 
-        def unit(k):
-            other = neigh[group, jnp.maximum(k - 1, 0), own]
-            return jnp.where(k == 0, GHOSTS + own, other), jnp.where(k == 0, spare, other)
-
-        twos = (high - low) // 2
-
-        def two_tiles(k, _):
-            (one, to_one), (two, to_two) = unit(low + 2 * k), unit(low + 2 * k + 1)
-            forces = pair(slot, [ext[group, one], ext[group, two]])
-            react[group, to_one] -= forces[0]
-            react[group, to_two] -= forces[1]
+        @pl.when((low == 0) & (high > 0))
+        def _():
+            items[0, size] = slot
+            items[1, size] = GHOSTS + own
+            items[2, size] = spare
+
+        def note(k, _):
+            other = neigh[group, k - 1, own]
+            items[0, size + k - low] = slot
+            items[1, size + k - low] = other
+            items[2, size + k - low] = other
             return 0
 
-        lax.fori_loop(0, twos, two_tiles, 0)
-
-        @pl.when(low + 2 * twos < high)
-        def _():
-            one, to_one = unit(high - 1)
-            react[group, to_one] -= pair(slot, [ext[group, one]])[0]
-
-        return start + tiles + BIN_COST
+        lax.fori_loop(jnp.maximum(low, 1), high, note, 0)
+        return start + tiles + BIN_COST, size + high - low
 
     def one_chunk(group, chunk, start):
         stop = start
@@ -232,7 +229,20 @@
             here = GHOSTS + chunk * CHUNK
             for slot in range(CHUNK):
                 fill_columns(slot, ext[group, here + slot])
-            lax.fori_loop(0, CHUNK, functools.partial(one_bin, group, chunk), start)
+            _, size = lax.fori_loop(
+                0, CHUNK, functools.partial(note_bin, group, chunk), (start, 0)
+            )
+
+            def two(k, _):
+                run(group, 2 * k, 2)
+                return 0
+
+            lax.fori_loop(0, size // 2, two, 0)
+
+            @pl.when(size % 2 == 1)
+            def _():
+                run(group, size - 1, 1)
+
             sums = [row_sums(slot) for slot in range(CHUNK)]
             for slot in range(CHUNK):
                 react[group, here + slot] += sums[slot]
@@ -369,6 +379,8 @@
             scratch_shapes=[
                 pltpu.VMEM((CHUNK, 5, spheres, spheres), jnp.float32),
                 pltpu.VMEM((CHUNK, 3, spheres, spheres), jnp.float32),
+                pltpu.VMEM((CHUNK, 3, spheres, spheres), jnp.float32),
+                pltpu.SMEM((3, CHUNK * (slots + 1)), jnp.int32),
                 pltpu.VMEM((3, bins, spheres), jnp.float32),
                 pltpu.SemaphoreType.DMA,
             ],

time: 45.4 us -> 47.5 us (1.046)
  Pallas kernels: 42.1 us -> 43.9 us
    pallas_call x1, Pallas kernels: 21.4 us -> 23.1 us  [local(): pl.pallas_call(functools.partial(tiles_kernel, sectors), out_shape=(jax.S...]
where the time goes in v3:
time: 47.5 us; the launch traced here: 47 us
  Pallas kernels  43.9 us (92%)
  local copies, waits for them, and re-layouts  2.42 us (5%)
  between operations  0.7 us (1%)
    pallas_call x1, Pallas kernels, local(): pl.pallas_call(functools.partial(tiles_kernel, sectors), out_shape=(jax.S...  23.1 us
    pallas_call x1, Pallas kernels, local(): pl.pallas_call(functools.partial(spread_kernel, slabs, sectors), out_shap...  11.4 us
    pallas_call x1, Pallas kernels, local(): pl.pallas_call(functools.partial(gather_kernel, slabs, sectors, bins), ou...  8.65 us
    unnamed x10, local copies, waits for them, and re-layouts  2.42 us

profile of v3, /device:TPU:0, one launch (start us, length us, event | category | flops | bytes accessed | tf_op | source)
XLA Modules:
  0.0 47.0 jit_solution(5747896318737751143)
XLA Ops:
  0.6 11.4 %shard_map.85 = (f32[4,48,4,128]{3,2,1,0:T(4,128)}, s32[4,16,32]{2,1,0:T(8,128)}, s32[4,1,32]{2,1,0:T(1,128)}, f32[3,32,128]{2,1,0:T(8,128)}, f32[32,128]{1,0:T(8,128)}) custom-call(f32[3,32,128]{2,1,0:T(8,128)} %bitcast.8, f32[32,128]{1,0:T(8,128)} %rad_in.1, f32[3,32,128]{2,1,0:T(8,128)} %bitcast.9, f32[3,32,128]{2,1,0:T(8,128)} %bitcast.10, ...), custom_call_target="tpu_custom_call" | custom-call | tf_op jit(solution)/shard_map/pallas_call | solution.py:344
  12.1 0.0 copy-start.4
  12.1 0.7 %copy-done.4 = s32[4,1,32]{2,1,0:T(1,128)S(1)} copy-done((s32[4,1,32]{2,1,0:T(1,128)S(1)}, s32[4,1,32]{2,1,0:T(1,128)}, u32[]{:S(2)}) %copy-start.4) | copy-done | bytes 536
  12.7 0.0 copy-start
  12.7 1.0 %copy-done = f32[4,48,4,128]{3,2,1,0:T(4,128)S(1)} copy-done((f32[4,48,4,128]{3,2,1,0:T(4,128)S(1)}, f32[4,48,4,128]{3,2,1,0:T(4,128)}, u32[]{:S(2)}) %copy-start) | copy-done | bytes 393240
  13.7 0.0 copy-start.2
  13.7 0.8 %copy-done.2 = s32[4,16,32]{2,1,0:T(8,128)S(1)} copy-done((s32[4,16,32]{2,1,0:T(8,128)S(1)}, s32[4,16,32]{2,1,0:T(8,128)}, u32[]{:S(2)}) %copy-start.2) | copy-done | bytes 8216
  14.5 23.1 %shard_map.86 = (f32[3,32,128]{2,1,0:T(8,128)}, f32[4,49,3,128]{3,2,1,0:T(4,128)S(1)}) custom-call(s32[4,16,32]{2,1,0:T(8,128)S(1)} %copy-done.2, s32[4,1,32]{2,1,0:T(1,128)S(1)} %copy-done.4, f32[4,48,4,128]{3,2,1,0:T(4,128)S(1)} %copy-done), custom_call_target="tpu_custom_call" | custom-call | tf_op jit(solution)/shard_map/pallas_call | solution.py:371
  37.6 0.0 copy-start.1
  37.6 0.0 copy-start.3
  37.6 8.7 %shard_map.87.force = f32[32,3,128]{2,1,0:T(4,128)S(1)} custom-call(f32[4,49,3,128]{3,2,1,0:T(4,128)S(1)} %get-tuple-element.16.react), custom_call_target="tpu_custom_call" | custom-call | tf_op jit(solution)/shard_map/pallas_call | solution.py:389
  46.3 0.0 copy-done.1
  46.3 0.0 copy-done.3
  46.3 0.7 %shard_map.88 = (f32[3,32,128]{2,1,0:T(8,128)}, f32[3,32,128]{2,1,0:T(8,128)}) custom-call(f32[32,3,128]{2,1,0:T(4,128)S(1)} %shard_map.87.force, f32[3,32,128]{2,1,0:T(8,128)S(1)} %copy-done.1, f32[32,128]{1,0:T(8,128)S(1)} %copy-done.3), custom_call_target="tpu_custom_call" | custom-call | tf_op jit(solution)/shard_map/pallas_call | solution.py:405
Async XLA Ops:
  12.1 0.7 %copy-start.4 = (s32[4,1,32]{2,1,0:T(1,128)S(1)}, s32[4,1,32]{2,1,0:T(1,128)}, u32[]{:S(2)}) copy-start(s32[4,1,32]{2,1,0:T(1,128)} %get-tuple-element.13.count) | copy-start | bytes 1540
  12.7 1.0 %copy-start = (f32[4,48,4,128]{3,2,1,0:T(4,128)S(1)}, f32[4,48,4,128]{3,2,1,0:T(4,128)}, u32[]{:S(2)}) copy-start(f32[4,48,4,128]{3,2,1,0:T(4,128)} %get-tuple-element.14.ext) | copy-start | bytes 1179652
  13.7 0.8 %copy-start.2 = (s32[4,16,32]{2,1,0:T(8,128)S(1)}, s32[4,16,32]{2,1,0:T(8,128)}, u32[]{:S(2)}) copy-start(s32[4,16,32]{2,1,0:T(8,128)} %get-tuple-element.12.neigh) | copy-start | bytes 24580
  37.6 8.7 %copy-start.1 = (f32[3,32,128]{2,1,0:T(8,128)S(1)}, f32[3,32,128]{2,1,0:T(8,128)}, u32[]{:S(2)}) copy-start(f32[3,32,128]{2,1,0:T(8,128)} %get-tuple-element.17.base) | copy-start | bytes 147460
  37.6 8.7 %copy-start.3 = (f32[32,128]{1,0:T(8,128)S(1)}, f32[32,128]{1,0:T(8,128)}, u32[]{:S(2)}) copy-start(f32[32,128]{1,0:T(8,128)} %get-tuple-element.18.mass) | copy-start | bytes 49156
